TPU v7x, 32 devices: a whole 2x2x4 slice. The times are simulated.
32 devices in a mesh: dp: 16 (over z, y, x), tensor: 2 (over core).
Axes of the slice: x: 2, y: 2, z: 4, core: 2. Of those that a mesh axis runs over, the one named last changes fastest.
Arguments:
- images: bfloat16 [160, 64, 768], P('dp', None, 'tensor'), may hold values from -6 to 6
- embedding: bfloat16 [160, 768], P('dp', 'tensor'), may hold values from -6 to 6
- counts: int32 [16], P('dp'), may hold values from 0 to 10, as said below
- norm_gains: float32 [3, 768], P(None, 'tensor'), may hold values from 0.5 to 1.5
- norm_shifts: float32 [3, 768], P(None, 'tensor'), may hold values from -3 to 3
- lin_biases: float32 [7, 768], P(None, 'tensor'), may hold values from -3 to 3
- conv_weights: bfloat16 [2, 9, 768, 768], P(None, None, 'dp', 'tensor'), may hold values from -0.078125 to 0.078125
- aff_weights: bfloat16 [768, 2, 768], P('dp', None, 'tensor'), may hold values from -0.21875 to 0.21875
- qkv_weights: bfloat16 [768, 3, 768], P('dp', None, 'tensor'), may hold values from -0.21875 to 0.21875
- proj_weights: bfloat16 [768, 768], P('dp', 'tensor'), may hold values from -1.75 to 1.75
- cotangent: float32 [160, 64, 768], P('dp', None, 'tensor'), may hold values from -6 to 6
Outputs:
- block_output: bfloat16 [160, 64, 768], P('dp', None, 'tensor')
- images_grad: bfloat16 [160, 64, 768], P('dp', None, 'tensor')
- embedding_grad: bfloat16 [160, 768], P('dp', 'tensor')
- gains_grad: float32 [3, 768], P(None, 'tensor')
- shifts_grad: float32 [3, 768], P(None, 'tensor')
- biases_grad: float32 [7, 768], P(None, 'tensor')
- conv_grad: float32 [2, 9, 768, 768], P(None, None, 'dp', 'tensor')
- aff_grad: float32 [768, 2, 768], P('dp', None, 'tensor')
- qkv_grad: float32 [768, 3, 768], P('dp', None, 'tensor')
- proj_grad: float32 [768, 768], P('dp', 'tensor')
Inputs may be any that keep to these rules, and one draw needn't show every extreme that they name: Device d of dp holds counts[d] real images, in its first counts[d] of 10 slots; some device holds 10.
All inputs are finite; a program needn't handle non-finite values.
Results may differ from a plain program's by a relative error of at most 0.02.
Values may be sent and summed in bfloat16 or wider, within the bound.
A program may use at most 192 MiB of HBM per device.

v0:
```python
import jax
import jax.numpy as jnp
from jax import lax
from jax.sharding import PartitionSpec as P

C = 768
HEAD_DIM = 64
GROUPS = 32
SIDE = 8
PIXELS = 64


def group_norm(values, gain_vec, shift_vec):
    batch_size = values.shape[0]
    grouped = values.reshape(batch_size, PIXELS, -1, C // GROUPS)
    centre = jnp.mean(grouped, axis=(1, 3), keepdims=True)
    spread = jnp.mean(jnp.square(grouped - centre), axis=(1, 3), keepdims=True)
    normal = ((grouped - centre) * lax.rsqrt(spread + 1e-05)).reshape(values.shape)
    return normal * gain_vec + shift_vec


def first_norm(values, gain_vec, shift_vec):
    return jax.nn.silu(group_norm(values, gain_vec, shift_vec))


def middle(conv_values, modulation, gain_vec, shift_vec):
    scaled = (
        group_norm(conv_values, gain_vec, shift_vec) * (1.0 + modulation[:, 0:1])
        + modulation[:, 1:2]
    )
    return jax.nn.silu(scaled)


def windows(source):
    slot_count = source.shape[0]
    padded = jnp.pad(source.reshape(slot_count, SIDE, SIDE, -1), ((0, 0), (1, 1), (1, 1), (0, 0)))
    found = []
    for tap_index in range(9):
        row_shift = tap_index // 3
        col_shift = tap_index % 3
        found.append(
            padded[:, row_shift : row_shift + SIDE, col_shift : col_shift + SIDE].reshape(
                slot_count * PIXELS, -1
            )
        )
    return found


def convolve(source, kernel):
    slot_count = source.shape[0]
    summed = jnp.zeros((slot_count * PIXELS, kernel.shape[2]), jnp.float32)
    for tap_index, window in enumerate(windows(source)):
        summed = summed + jnp.dot(window, kernel[tap_index], preferred_element_type=jnp.float32)
    return summed.reshape(slot_count, PIXELS, -1)


def convolve_back(grad_low, kernel):
    slot_count = grad_low.shape[0]
    flattened = grad_low.reshape(slot_count * PIXELS, -1)
    summed = jnp.zeros((slot_count, SIDE + 2, SIDE + 2, kernel.shape[1]), jnp.float32)
    for tap_index in range(9):
        row_shift = tap_index // 3
        col_shift = tap_index % 3
        contrib = jnp.einsum(
            "rd,cd->rc", flattened, kernel[tap_index], preferred_element_type=jnp.float32
        )
        contrib = contrib.reshape(slot_count, SIDE, SIDE, -1)
        summed = summed + jnp.pad(
            contrib, ((0, 0), (row_shift, 2 - row_shift), (col_shift, 2 - col_shift), (0, 0))
        )
    return summed[:, 1 : SIDE + 1, 1 : SIDE + 1].reshape(slot_count, PIXELS, -1)


def conv_weight_grad(source, grad_low):
    slot_count = source.shape[0]
    flattened = grad_low.reshape(slot_count * PIXELS, -1)
    found = [
        jnp.einsum("rc,rd->cd", window, flattened, preferred_element_type=jnp.float32)
        for window in windows(source)
    ]
    return jnp.stack(found)


def gather_features(values_low):
    return lax.all_gather(values_low, "tensor", axis=2, tiled=True)


def back_features(partial_sum):
    return lax.psum_scatter(
        partial_sum.astype(jnp.bfloat16), "tensor", scatter_dimension=2, tiled=True
    ).astype(jnp.float32)


def body(
    images,
    embedding,
    counts,
    norm_gains,
    norm_shifts,
    lin_biases,
    conv_weights,
    aff_weights,
    qkv_weights,
    proj_weights,
    cotangent,
):
    slot_count = images.shape[0]
    score_scale = HEAD_DIM ** (-0.5)
    slot_mask = (jnp.arange(slot_count, dtype=jnp.int32) < counts[0]).astype(jnp.float32)
    conv_full = lax.all_gather(conv_weights, "dp", axis=2, tiled=True)
    aff_full, qkv_full, proj_full = (
        lax.all_gather(aff_weights, "dp", axis=0, tiled=True),
        lax.all_gather(qkv_weights, "dp", axis=0, tiled=True),
        lax.all_gather(proj_weights, "dp", axis=0, tiled=True),
    )
    images_f = images.astype(jnp.float32)
    hidden0 = first_norm(images_f, norm_gains[0], norm_shifts[0]).astype(jnp.bfloat16)
    hidden0_all, embed_all = (
        lax.all_gather(hidden0, "tensor", axis=2, tiled=True),
        lax.all_gather(embedding, "tensor", axis=1, tiled=True),
    )
    conv_out0 = convolve(hidden0_all, conv_full[0]) + lin_biases[0]
    modulation = (
        jnp.einsum("sc,cjd->sjd", embed_all, aff_full, preferred_element_type=jnp.float32)
        + lin_biases[5:7]
    )
    hidden1 = middle(conv_out0, modulation, norm_gains[1], norm_shifts[1]).astype(jnp.bfloat16)
    hidden1_all = gather_features(hidden1)
    residual = images_f + (convolve(hidden1_all, conv_full[1]) + lin_biases[1])
    normed = group_norm(residual, norm_gains[2], norm_shifts[2]).astype(jnp.bfloat16)
    normed_all = gather_features(normed)
    bias_rows = jnp.stack([lin_biases[2], jnp.zeros_like(lin_biases[2]), lin_biases[3]])
    projected = (
        jnp.einsum("spc,cjd->spjd", normed_all, qkv_full, preferred_element_type=jnp.float32)
        + bias_rows
    ).astype(jnp.bfloat16)
    head_shape = (slot_count, PIXELS, -1, HEAD_DIM)
    query_heads = projected[:, :, 0].reshape(head_shape)
    key_heads = projected[:, :, 1].reshape(head_shape)
    value_heads = projected[:, :, 2].reshape(head_shape)
    scores = (
        jnp.einsum("sqhd,skhd->shqk", query_heads, key_heads, preferred_element_type=jnp.float32)
        * score_scale
    )
    log_total = jax.scipy.special.logsumexp(scores, axis=-1, keepdims=True)
    probabilities = jnp.exp(scores - log_total)
    weights_low = probabilities.astype(jnp.bfloat16)
    attended = jnp.einsum(
        "shqk,skhd->sqhd", weights_low, value_heads, preferred_element_type=jnp.float32
    )
    attended = attended.reshape(slot_count, PIXELS, -1).astype(jnp.bfloat16)
    attended_all = gather_features(attended)
    branch = (
        jnp.einsum("spc,cd->spd", attended_all, proj_full, preferred_element_type=jnp.float32)
        + lin_biases[4]
    )
    block_output = (slot_mask[:, None, None] * (residual + branch)).astype(jnp.bfloat16)
    conv_back = lax.all_gather(conv_weights, "dp", axis=2, tiled=True)
    aff_back, qkv_back, proj_back = (
        lax.all_gather(aff_weights, "dp", axis=0, tiled=True),
        lax.all_gather(qkv_weights, "dp", axis=0, tiled=True),
        lax.all_gather(proj_weights, "dp", axis=0, tiled=True),
    )
    grad_branch = slot_mask[:, None, None] * cotangent
    branch_low = grad_branch.astype(jnp.bfloat16)
    proj_grad = jnp.einsum(
        "spc,spd->cd", attended_all, branch_low, preferred_element_type=jnp.float32
    )
    proj_bias_grad = jnp.sum(branch_low.astype(jnp.float32), axis=(0, 1))
    attended_grad = back_features(
        jnp.einsum("spd,cd->spc", branch_low, proj_back, preferred_element_type=jnp.float32)
    )
    attended_low = attended_grad.astype(jnp.bfloat16).reshape(head_shape)
    grad_probs = jnp.einsum(
        "sqhd,skhd->shqk", attended_low, value_heads, preferred_element_type=jnp.float32
    )
    value_grad = jnp.einsum(
        "shqk,sqhd->skhd", weights_low, attended_low, preferred_element_type=jnp.float32
    )
    score_grad = probabilities * (
        grad_probs - jnp.sum(grad_probs * probabilities, axis=-1, keepdims=True)
    )
    score_low = score_grad.astype(jnp.bfloat16)
    query_grad = (
        jnp.einsum("shqk,skhd->sqhd", score_low, key_heads, preferred_element_type=jnp.float32)
        * score_scale
    )
    key_grad = (
        jnp.einsum("shqk,sqhd->skhd", score_low, query_heads, preferred_element_type=jnp.float32)
        * score_scale
    )
    flat_shape = (slot_count, PIXELS, -1)
    projected_grad = jnp.stack(
        [
            query_grad.reshape(flat_shape),
            key_grad.reshape(flat_shape),
            value_grad.reshape(flat_shape),
        ],
        axis=2,
    ).astype(jnp.bfloat16)
    qkv_grad = jnp.einsum(
        "spc,spjd->cjd", normed_all, projected_grad, preferred_element_type=jnp.float32
    )
    qkv_bias_grad = jnp.sum(projected_grad.astype(jnp.float32), axis=(0, 1))
    normed_grad = back_features(
        jnp.einsum("spjd,cjd->spc", projected_grad, qkv_back, preferred_element_type=jnp.float32)
    )
    norm_value, norm_pull = jax.vjp(group_norm, residual, norm_gains[2], norm_shifts[2])
    residual_grad, gain2_grad, shift2_grad = norm_pull(normed_grad)
    residual_grad = residual_grad + grad_branch
    conv1_low = residual_grad.astype(jnp.bfloat16)
    conv1_bias_grad = jnp.sum(conv1_low.astype(jnp.float32), axis=(0, 1))
    conv1_wgrad = conv_weight_grad(hidden1_all, conv1_low)
    hidden1_grad = back_features(convolve_back(conv1_low, conv_back[1]))
    middle_value, middle_pull = jax.vjp(
        middle, conv_out0, modulation, norm_gains[1], norm_shifts[1]
    )
    conv0_grad, modulation_grad, gain1_grad, shift1_grad = middle_pull(hidden1_grad)
    modulation_low = modulation_grad.astype(jnp.bfloat16)
    aff_bias_grad = jnp.sum(modulation_low.astype(jnp.float32), axis=0)
    aff_grad = jnp.einsum(
        "sc,sjd->cjd", embed_all, modulation_low, preferred_element_type=jnp.float32
    )
    embed_part = jnp.einsum(
        "sjd,cjd->sc", modulation_low, aff_back, preferred_element_type=jnp.float32
    )
    conv0_low = conv0_grad.astype(jnp.bfloat16)
    conv0_bias_grad = jnp.sum(conv0_low.astype(jnp.float32), axis=(0, 1))
    conv0_wgrad = conv_weight_grad(hidden0_all, conv0_low)
    hidden0_part = convolve_back(conv0_low, conv_back[0])
    hidden0_grad, embedding_sum = (
        lax.psum_scatter(
            hidden0_part.astype(jnp.bfloat16), "tensor", scatter_dimension=2, tiled=True
        ).astype(jnp.float32),
        lax.psum_scatter(
            embed_part.astype(jnp.bfloat16), "tensor", scatter_dimension=1, tiled=True
        ).astype(jnp.float32),
    )
    first_value, first_pull = jax.vjp(first_norm, images_f, norm_gains[0], norm_shifts[0])
    images_part, gain0_grad, shift0_grad = first_pull(hidden0_grad)
    images_grad = (images_part + residual_grad).astype(jnp.bfloat16)
    gains_local = jnp.stack([gain0_grad, gain1_grad, gain2_grad])
    shifts_local = jnp.stack([shift0_grad, shift1_grad, shift2_grad])
    biases_local = jnp.stack(
        [
            conv0_bias_grad,
            conv1_bias_grad,
            qkv_bias_grad[0],
            qkv_bias_grad[2],
            proj_bias_grad,
            aff_bias_grad[0],
            aff_bias_grad[1],
        ]
    )
    gains_grad, shifts_grad, biases_grad = lax.psum((gains_local, shifts_local, biases_local), "dp")
    conv_local = jnp.stack([conv0_wgrad, conv1_wgrad])
    conv_summed, aff_summed, qkv_summed, proj_summed = (
        lax.psum_scatter(conv_local, "dp", scatter_dimension=2, tiled=True),
        lax.psum_scatter(aff_grad, "dp", scatter_dimension=0, tiled=True),
        lax.psum_scatter(qkv_grad, "dp", scatter_dimension=0, tiled=True),
        lax.psum_scatter(proj_grad, "dp", scatter_dimension=0, tiled=True),
    )
    return (
        block_output,
        images_grad,
        embedding_sum.astype(jnp.bfloat16),
        gains_grad,
        shifts_grad,
        biases_grad,
        conv_summed,
        aff_summed,
        qkv_summed,
        proj_summed,
    )


def solution(mesh):
    return jax.shard_map(
        body,
        mesh=mesh,
        in_specs=(
            P("dp", None, "tensor"),
            P("dp", "tensor"),
            P("dp"),
            P(None, "tensor"),
            P(None, "tensor"),
            P(None, "tensor"),
            P(None, None, "dp", "tensor"),
            P("dp", None, "tensor"),
            P("dp", None, "tensor"),
            P("dp", "tensor"),
            P("dp", None, "tensor"),
        ),
        out_specs=(
            P("dp", None, "tensor"),
            P("dp", None, "tensor"),
            P("dp", "tensor"),
            P(None, "tensor"),
            P(None, "tensor"),
            P(None, "tensor"),
            P(None, None, "dp", "tensor"),
            P("dp", None, "tensor"),
            P("dp", None, "tensor"),
            P("dp", "tensor"),
        ),
        check_vma=False,
    )
```

profile of v0, /device:TPU:0, one launch (start us, length us, event | category | flops | bytes accessed | tf_op | source)
XLA Modules:
  0.0 1100.9 jit_solution(12496315842939476462)
XLA Ops:
  8.7 45.9 %all_gather.39 = bf16[768,384]{1,0:T(8,128)(2,1)S(1)} all-gather(bf16[48,384]{1,0:T(8,128)(2,1)} %param.20), channel_id=1, replica_groups=mesh['dp'=16,'tensor'=2] {'dp'}, dimensions={0}, use_global_device_ids=true | all-gather | bytes 626688 | tf_op jit(solution)/shard_map/all_gather | solution.py:114
  58.3 3.8 copy.194
  62.1 4.7 reshape.489
  76.2 3.0 pad_slice_fusion.8
  82.9 39.7 %all-gather.6.cloned.1.call-done = bf16[768,2,384]{2,0,1:T(8,128)(2,1)} async-done(((bf16[48,2,384]{2,0,1:T(8,128)(2,1)}), bf16[768,2,384]{2,0,1:T(8,128)(2,1)}) %all-gather.6.cloned.1.call-update) | async-done | bytes 1179664 | tf_op jit(solution)/shard_map/all_gather | solution.py:112
  124.2 132.7 %all-gather.4.cloned.1.call-done = bf16[2,9,768,384]{3,2,1,0:T(8,128)(2,1)} async-done(((bf16[2,9,48,384]{3,2,1,0:T(8,128)(2,1)}), bf16[2,9,768,384]{3,2,1,0:T(8,128)(2,1)}) %all-gather.4.cloned.1.call-update) | async-done | bytes 10616848 | tf_op jit(solution)/shard_map/all_gather | solution.py:110
  304.2 2.8 all_gather.36
  307.0 10.0 all-gather.8.cloned.1.call-done
  317.0 2.9 add_convert_fusion
  336.0 3.1 copy.153
  339.1 3.2 stack_reshape.12
  342.3 3.0 copy.157
  348.0 4.2 bitcast_convert_fusion
  352.2 4.9 copy.196
  357.1 4.6 reshape.491
  361.8 7.1 reduce-scatter.27.cloned.1.call-done
  368.9 2.9 reshape.492
  412.5 3.8 copy.198
  416.3 5.0 reshape.493
  421.3 9.7 reduce-scatter.29.cloned.1.call-done
  436.4 3.8 multiply_reduce_fusion.4
  468.8 4.9 copy.200
  473.8 4.6 reshape.495
  480.4 5.3 copy.165
  485.8 3.0 convolution_convert_fusion.2
  496.1 4.7 convolution_bitcast_fusion
  518.1 7.7 pad_maximum_fusion
  538.7 3.3 fusion.57
  546.1 77.9 %all-reduce.23 = (f32[3,384]{1,0:T(4,128)}, f32[3,384]{1,0:T(4,128)}, f32[7,384]{1,0:T(8,128)}) all-reduce(f32[3,384]{1,0:T(4,128)S(1)} %pad_maximum_fusion.3, f32[3,384]{1,0:T(4,128)S(1)} %pad_maximum_fusion.4, f32[7,384]{1,0:T(8,128)} %stack.126), channel_id=1, replica_groups=mesh['dp'=16,'tensor'=2] {'dp'}, use_global_device_ids=true, to_apply=%region_40.41 | all-reduce | flops 4992 | bytes 39936 | tf_op jit(solution)/shard_map/psum | solution.py:255
  628.3 6.7 reduce-scatter.23.cloned.1.call-done
  635.1 138.2 %reduce-scatter.21.cloned.1.call-done = f32[48,3,384]{2,0,1:T(8,128)} async-done(((f32[768,3,384]{2,0,1:T(8,128)}), f32[48,3,384]{2,0,1:T(8,128)}) %reduce-scatter.21.cloned.1.call-update) | async-done | bytes 221200 | tf_op jit(solution)/shard_map/reduce_scatter | solution.py:260
  773.2 319.8 %reduce-scatter.19.cloned.1.call-done = f32[2,9,48,384]{3,2,1,0:T(8,128)} async-done(((f32[2,9,768,384]{3,2,1,0:T(8,128)}), f32[2,9,48,384]{3,2,1,0:T(8,128)}) %reduce-scatter.19.cloned.1.call-update) | async-done | bytes 1327120 | tf_op jit(solution)/shard_map/reduce_scatter | solution.py:258
  (455 shorter events, 204.4 us)
Async XLA Ops:
  8.0 72.2 %reduce-scatter.25.cloned.1.call-start = ((), (), s32[]{:S(2)}) async-start(), calls=%async_computation.14 | async-start | bytes 1474560
  8.7 48.1 %copy-start.106 = (f32[10]{0:T(128)}, f32[10]{0:T(128)S(1)}, u32[]{:S(2)}) copy-start(f32[10]{0:T(128)S(1)} %compare_convert_fusion) | copy-start | bytes 124
  66.8 55.8 %all-gather.6.cloned.1.call-start = ((), (), s32[]{:S(2)}) async-start(), calls=%async_computation.9 | async-start | bytes 1253376 | tf_op jit(solution)/shard_map/all_gather | solution.py:112
  67.5 189.3 %all-gather.4.cloned.1.call-start = ((), (), s32[]{:S(2)}) async-start(), calls=%async_computation.8 | async-start | bytes 11280384 | tf_op jit(solution)/shard_map/all_gather | solution.py:110
  68.1 248.9 %all-gather.8.cloned.1.call-start = ((), (), s32[]{:S(2)}) async-start(), calls=%async_computation.10 | async-start | bytes 1880064 | tf_op jit(solution)/shard_map/all_gather | solution.py:113
  68.7 300.2 %reduce-scatter.27.cloned.1.call-start = ((), (), s32[]{:S(2)}) async-start(), calls=%async_computation.15 | async-start | bytes 1474560
  69.4 210.6 %copy-start.87 = (f32[384]{0:T(512)}, f32[384]{0:T(512)S(1)}, u32[]{:S(2)}) copy-start(f32[384]{0:T(512)S(1)} %get-tuple-element.46) | copy-start | bytes 4612
  69.5 208.7 %copy-start.77 = (f32[16,24]{1,0:T(8,128)}, f32[16,24]{1,0:T(8,128)S(1)}, u32[]{:S(2)}) copy-start(f32[16,24]{1,0:T(8,128)S(1)} %add.355) | copy-start | bytes 4612
  71.3 51.3 %copy-start.74 = (bf16[10,768]{1,0:T(8,128)(2,1)}, bf16[10,768]{1,0:T(8,128)(2,1)S(1)}, u32[]{:S(2)}) copy-start(bf16[10,768]{1,0:T(8,128)(2,1)S(1)} %all_gather.33) | copy-start | bytes 46084
  73.1 206.9 %copy-start.91 = (f32[384]{0:T(512)}, f32[384]{0:T(512)S(1)}, u32[]{:S(2)}) copy-start(f32[384]{0:T(512)S(1)} %get-tuple-element.95) | copy-start | bytes 4612
  73.1 206.9 %copy-start.93 = (f32[384]{0:T(512)}, f32[384]{0:T(512)S(1)}, u32[]{:S(2)}) copy-start(f32[384]{0:T(512)S(1)} %get-tuple-element.52) | copy-start | bytes 4612
  76.2 188.3 %copy-start.9 = (bf16[10,64,768]{2,1,0:T(8,128)(2,1)}, bf16[10,64,768]{2,1,0:T(8,128)(2,1)S(1)}, u32[]{:S(2)}) copy-start(bf16[10,64,768]{2,1,0:T(8,128)(2,1)S(1)} %all_gather.31) | copy-start | bytes 2949124
  79.2 190.7 %copy-start.21 = (bf16[10,8,8,768]{3,2,1,0:T(8,128)(2,1)}, bf16[10,8,8,768]{3,2,1,0:T(8,128)(2,1)S(1)}, u32[]{:S(2)}) copy-start(bf16[10,8,8,768]{3,2,1,0:T(8,128)(2,1)S(1)} %get-tuple-element.83) | copy-start | bytes 2949124
  79.3 192.4 %copy-start.19 = (bf16[10,8,8,768]{3,2,1,0:T(8,128)(2,1)}, bf16[10,8,8,768]{3,2,1,0:T(8,128)(2,1)S(1)}, u32[]{:S(2)}) copy-start(bf16[10,8,8,768]{3,2,1,0:T(8,128)(2,1)S(1)} %get-tuple-element.77) | copy-start | bytes 2949124
  124.2 155.8 %copy-start.76 = (f32[10,384]{1,0:T(8,128)}, f32[10,384]{1,0:T(8,128)S(1)}, u32[]{:S(2)}) copy-start(f32[10,384]{1,0:T(8,128)S(1)} %get-tuple-element.86) | copy-start | bytes 46084
  303.0 89.5 %copy-start.1 = (f32[10,64,384]{2,1,0:T(8,128)}, f32[10,64,384]{2,1,0:T(8,128)S(1)}, u32[]{:S(2)}) copy-start(f32[10,64,384]{2,1,0:T(8,128)S(1)} %get-tuple-element.65) | copy-start | bytes 2949124
  303.4 89.0 %copy-start.60 = (f32[10,384]{1,0:T(8,128)}, f32[10,384]{1,0:T(8,128)S(1)}, u32[]{:S(2)}) copy-start(f32[10,384]{1,0:T(8,128)S(1)} %sub.131) | copy-start | bytes 46084
  304.0 88.5 %copy-start.66 = (f32[10,384]{1,0:T(8,128)}, f32[10,384]{1,0:T(8,128)S(1)}, u32[]{:S(2)}) copy-start(f32[10,384]{1,0:T(8,128)S(1)} %mul.352) | copy-start | bytes 46084
  361.8 69.3 %reduce-scatter.29.cloned.1.call-start = ((), (), s32[]{:S(2)}) async-start(), calls=%async_computation.16 | async-start | bytes 1474560
  374.0 16.8 %copy-start.17 = (bf16[10,64,384]{2,1,0:T(8,128)(2,1)}, bf16[10,64,384]{2,1,0:T(8,128)(2,1)S(1)}, u32[]{:S(2)}) copy-start(bf16[10,64,384]{2,1,0:T(8,128)(2,1)S(1)} %copy.197) | copy-start | bytes 1474564
  421.3 112.5 %reduce-scatter.33.cloned.1.call-start = ((), (), s32[]{:S(2)}) async-start(), calls=%async_computation.18 | async-start | bytes 294912
  447.7 87.7 %reduce-scatter.31.cloned.1.call-start = ((), (), s32[]{:S(2)}) async-start(), calls=%async_computation.17 | async-start | bytes 1474560
  478.4 148.3 %all-reduce.26.cloned.1.call-start = ((), (), s32[]{:S(2)}) async-start(), calls=%async_computation.19 | async-start | bytes 4718592
  485.8 149.3 %reduce-scatter.23.cloned.1.call-start = ((), (), s32[]{:S(2)}) async-start(), calls=%async_computation.13 | async-start | bytes 1253376 | tf_op jit(solution)/shard_map/reduce_scatter | solution.py:261
  495.8 277.4 %reduce-scatter.21.cloned.1.call-start = ((), (), s32[]{:S(2)}) async-start(), calls=%async_computation.12 | async-start | bytes 3760128 | tf_op jit(solution)/shard_map/reduce_scatter | solution.py:260
  500.8 592.3 %reduce-scatter.19.cloned.1.call-start = ((), (), s32[]{:S(2)}) async-start(), calls=%async_computation.11 | async-start | bytes 22560768 | tf_op jit(solution)/shard_map/reduce_scatter | solution.py:258
  538.6 85.3 %copy-start.8 = (f32[10,64,384]{2,1,0:T(8,128)S(1)}, f32[10,64,384]{2,1,0:T(8,128)}, u32[]{:S(2)}) copy-start(f32[10,64,384]{2,1,0:T(8,128)} %param.21) | copy-start | bytes 2949124
  538.6 85.3 %copy-start.18 = (bf16[10,64,384]{2,1,0:T(8,128)(2,1)S(1)}, bf16[10,64,384]{2,1,0:T(8,128)(2,1)}, u32[]{:S(2)}) copy-start(bf16[10,64,384]{2,1,0:T(8,128)(2,1)} %copy-done.17) | copy-start | bytes 1474564
  538.7 85.3 %copy-start.61 = (f32[10,384]{1,0:T(8,128)S(1)}, f32[10,384]{1,0:T(8,128)}, u32[]{:S(2)}) copy-start(f32[10,384]{1,0:T(8,128)} %copy-done.60) | copy-start | bytes 46084
  538.7 85.3 %copy-start.67 = (f32[10,384]{1,0:T(8,128)S(1)}, f32[10,384]{1,0:T(8,128)}, u32[]{:S(2)}) copy-start(f32[10,384]{1,0:T(8,128)} %copy-done.66) | copy-start | bytes 46084
  538.7 85.3 %copy-start.69 = (f32[10,384]{1,0:T(8,128)S(1)}, f32[10,384]{1,0:T(8,128)}, u32[]{:S(2)}) copy-start(f32[10,384]{1,0:T(8,128)} %copy-done.68) | copy-start | bytes 46084
  538.7 85.3 %copy-start.86 = (f32[384]{0:T(512)S(1)}, f32[384]{0:T(512)}, u32[]{:S(2)}) copy-start(f32[384]{0:T(512)} %get-tuple-element.97) | copy-start | bytes 4612
  (92 other events, 403.8 us)
Sparse Core Ops, SparseCore 0:
  66.9 4.3 reduce-scatter.24
  361.9 6.9 reduce-scatter.26
  421.4 9.6 reduce-scatter.28
  447.8 8.7 reduce-scatter.32
  478.5 9.6 reduce-scatter.30
  495.9 139.0 reduce-scatter.22
  640.7 132.4 reduce-scatter.20
  779.8 313.2 reduce-scatter.18
Sparse Core Ops, SparseCore 1:
  70.5 52.0 all-gather.5
  125.2 131.6 all-gather.3
  259.4 57.5 all-gather.7
  485.9 135.7 all-reduce.25
where the time goes:
time: 1110 us; the launch traced here: 1100 us
  waiting for transfers between devices  665 us (60%)
  blocking collectives  136 us (12%)
  local copies, waits for them, and re-layouts  116 us (10%)
  matrix products  112 us (10%)
  other arithmetic  50.9 us (5%)
  between operations  19.4 us (2%)
    reduce_scatter x1, waiting for transfers between devices, body(): lax.psum_scatter(conv_local, 'dp', scatter_dimension=2, tiled=True)  320 us
    reduce_scatter x1, waiting for transfers between devices, body(): lax.psum_scatter(qkv_grad, 'dp', scatter_dimension=0, tiled=True)  138 us
    all_gather x1, waiting for transfers between devices, body(): conv_full = lax.all_gather(conv_weights, 'dp', axis=2, tiled=True)  133 us
    psum x1, blocking collectives, body(): lax.psum((gains_local, shifts_local, biases_local), 'dp')  77.9 us
    unnamed x244, local copies, waits for them, and re-layouts  65.2 us
    all_gather x1, blocking collectives, body(): lax.all_gather(proj_weights, 'dp', axis=0, tiled=True)  45.9 us
    all_gather x1, waiting for transfers between devices, body(): lax.all_gather(aff_weights, 'dp', axis=0, tiled=True)  39.7 us
    dot_general x18, matrix products, convolve(): jnp.dot(window, kernel[tap_index], preferred_element_type=jnp.float32)  32.9 us
  transfers between devices with their start and end apart: 12, of which 8 were waited for; matrix products, arithmetic and copies ran while one was open for 13% of the time, Pallas kernels for 0%

commit v1 on v0

--- a/solution.py
+++ b/solution.py
@@ -1,13 +1,193 @@
+import functools
+
 import jax
 import jax.numpy as jnp
 from jax import lax
+from jax.experimental import pallas as pl
+from jax.experimental.pallas import tpu as pltpu
 from jax.sharding import PartitionSpec as P
+
+MESH = pl.DeviceIdType.MESH
+GRID = (4, 2, 2)
 
 C = 768
 HEAD_DIM = 64
 GROUPS = 32
 SIDE = 8
 PIXELS = 64
+
+
+def piece_columns(width):
+    convs = [(part * 3 * width, 3 * width) for part in range(6)]
+    return convs[:3] + [(18 * width, 2 * width)] + convs[3:] + [(20 * width, 3 * width), (23 * width, width)]
+
+
+def place():
+    spot = lax.axis_index("dp")
+    return spot, spot // 4, lax.rem(spot // 2, 2), lax.rem(spot, 2)
+
+
+def gather_kernel(pieces, conv_ref, aff_ref, qkv_ref, proj_ref, full_ref, own_sem, zsend, zrecv, fsend, frecv, ssend, srecv):
+    spot, z, y, x = place()
+    width = conv_ref.shape[3]
+    barrier = pltpu.get_barrier_semaphore()
+    line = [lax.rem(z + j, 4) * 4 + y * 2 + x for j in (1, 2, 3)]
+    xmate, ymate = z * 4 + y * 2 + 1 - x, z * 4 + (1 - y) * 2 + x
+    for mate in line + [xmate, ymate]:
+        pl.semaphore_signal(barrier, inc=1, device_id={"dp": mate}, device_id_type=MESH)
+    own = []
+    for tap in range(18):
+        own.append(pltpu.make_async_copy(conv_ref.at[tap // 9, tap % 9], full_ref.at[z, y, x, :, pl.ds(tap * width, width)], own_sem.at[tap]))
+    for at, (ref, start, size) in enumerate(((aff_ref, 18, 2), (qkv_ref, 20, 3), (proj_ref, 23, 1))):
+        own.append(pltpu.make_async_copy(ref, full_ref.at[z, y, x, :, pl.ds(start * width, size * width)], own_sem.at[18 + at]))
+    for copy in own:
+        copy.start()
+    for copy in own:
+        copy.wait()
+    pl.semaphore_wait(barrier, 5)
+
+    def remote(at, send, recv, mate):
+        return pltpu.make_async_remote_copy(src_ref=at, dst_ref=at, send_sem=send, recv_sem=recv, device_id={"dp": mate}, device_id_type=MESH)
+
+    started = {}
+
+    def stage(p, s):
+        cols = pl.ds(*pieces[p])
+        if s == 0:
+            block = full_ref.at[z, y, x, :, cols]
+            copies = [remote(block, zsend.at[p, j], zrecv.at[p, j], line[j]) for j in range(3)]
+        else:
+            for copy in started[p, s - 1]:
+                copy.wait_recv()
+            if s == 1:
+                block = full_ref.at[:, y, x, :, cols]
+                copies = [remote(block, fsend.at[p], frecv.at[p], ymate if p % 2 else xmate)]
+            elif s == 2:
+                block = full_ref.at[:, :, x, :, cols] if p % 2 else full_ref.at[:, y, :, :, cols]
+                copies = [remote(block, ssend.at[p], srecv.at[p], xmate if p % 2 else ymate)]
+            else:
+                copies = []
+        for copy in copies:
+            copy.start()
+        started[p, s] = copies
+
+    for step in range(len(pieces) + 3):
+        for p in range(len(pieces)):
+            if 0 <= step - p <= 3:
+                stage(p, step - p)
+    for copies in started.values():
+        for copy in copies:
+            copy.wait_send()
+
+
+def gather_weights(conv, aff, qkv, proj):
+    rows, width = conv.shape[2], conv.shape[3]
+    pieces = piece_columns(width)
+    n = len(pieces)
+    dma = pltpu.SemaphoreType.DMA
+    full = pl.pallas_call(
+        functools.partial(gather_kernel, pieces),
+        out_shape=jax.ShapeDtypeStruct(GRID + (rows, 24 * width), jnp.bfloat16),
+        in_specs=[pl.BlockSpec(memory_space=pl.ANY)] * 4,
+        out_specs=pl.BlockSpec(memory_space=pl.ANY),
+        scratch_shapes=[dma((21,)), dma((n, 3)), dma((n, 3)), dma((n,)), dma((n,)), dma((n,)), dma((n,))],
+        compiler_params=pltpu.CompilerParams(collective_id=0, has_side_effects=True),
+    )(conv, aff.reshape(rows, -1), qkv.reshape(rows, -1), proj)
+    return full
+
+
+def scatter_kernel(pieces, grad_ref, small_ref, out_ref, total_ref, work, r1, r2, r3, smalls, in_sem, sem1, sem2, sem3, small_sem):
+    spot, z, y, x = place()
+    barrier = pltpu.get_barrier_semaphore()
+    everyone = [lax.rem(spot + j, 16) for j in range(1, 16)]
+    line = [lax.rem(z + j, 4) for j in (1, 2, 3)]
+    xmate, ymate = z * 4 + y * 2 + 1 - x, z * 4 + (1 - y) * 2 + x
+    for mate in everyone:
+        pl.semaphore_signal(barrier, inc=1, device_id={"dp": mate}, device_id_type=MESH)
+    loads = []
+    for p, (start, size) in enumerate(pieces):
+        cols = pl.ds(start, size)
+        loads.append(pltpu.make_async_copy(grad_ref.at[:, :, :, :, cols], work.at[:, :, :, :, cols], in_sem.at[p]))
+        loads[-1].start()
+    pl.semaphore_wait(barrier, 15)
+
+    def remote(src, dst, send, recv, mate):
+        copy = pltpu.make_async_remote_copy(src_ref=src, dst_ref=dst, send_sem=send, recv_sem=recv, device_id={"dp": mate}, device_id_type=MESH)
+        copy.start()
+        return copy
+
+    small_copies = [remote(small_ref, smalls.at[spot], small_sem.at[0, j], small_sem.at[1, j], mate) for j, mate in enumerate(everyone)]
+    smalls[spot] = small_ref[...]
+    started = {}
+
+    def stage(p, s):
+        cols = pl.ds(*pieces[p])
+        odd = p % 2
+        copies = []
+        if s == 0:
+            loads[p].wait()
+            block = work.at[:, 1 - y, :, :, cols] if odd else work.at[:, :, 1 - x, :, cols]
+            copies = [remote(block, r1.at[:, :, :, cols], sem1.at[0, p], sem1.at[1, p], ymate if odd else xmate)]
+        elif s == 1:
+            for copy in started[p, 0]:
+                copy.wait_recv()
+            for zz in range(4):
+                for other in range(2):
+                    spot_now = (zz, y, other) if odd else (zz, other, x)
+                    total = work[spot_now + (slice(None), cols)].astype(jnp.float32) + r1[zz, other, :, cols].astype(jnp.float32)
+                    work[spot_now + (slice(None), cols)] = total.astype(jnp.bfloat16)
+            block = work.at[:, y, 1 - x, :, cols] if odd else work.at[:, 1 - y, x, :, cols]
+            copies = [remote(block, r2.at[:, :, cols], sem2.at[0, p], sem2.at[1, p], xmate if odd else ymate)]
+        elif s == 2:
+            for copy in started[p, 1]:
+                copy.wait_recv()
+            for zz in range(4):
+                total = work[zz, y, x, :, cols].astype(jnp.float32) + r2[zz, :, cols].astype(jnp.float32)
+                work[zz, y, x, :, cols] = total.astype(jnp.bfloat16)
+            copies = [remote(work.at[zz, y, x, :, cols], r3.at[j, :, cols], sem3.at[0, p, j], sem3.at[1, p, j], zz * 4 + y * 2 + x) for j, zz in enumerate(line)]
+        else:
+            for copy in started[p, 2]:
+                copy.wait_recv()
+            total = work[z, y, x, :, cols].astype(jnp.float32)
+            for j in range(3):
+                total = total + r3[j, :, cols].astype(jnp.float32)
+            out_ref[:, cols] = total
+        started[p, s] = copies
+
+    for step in range(len(pieces) + 3):
+        for p in range(len(pieces)):
+            if 0 <= step - p <= 3:
+                stage(p, step - p)
+    for copy in small_copies:
+        copy.wait_recv()
+    total_ref[...] = jnp.sum(smalls[...], axis=0)
+    for copies in list(started.values()) + [small_copies]:
+        for copy in copies:
+            copy.wait_send()
+
+
+def scatter_grads(grad, small):
+    rows, columns = grad.shape[3:]
+    pieces = piece_columns(columns // 24)
+    n = len(pieces)
+    dma = pltpu.SemaphoreType.DMA
+    low = jnp.bfloat16
+    vmem = pl.BlockSpec(memory_space=pltpu.VMEM)
+    return pl.pallas_call(
+        functools.partial(scatter_kernel, pieces),
+        out_shape=(jax.ShapeDtypeStruct((rows, columns), jnp.float32), jax.ShapeDtypeStruct(small.shape, jnp.float32)),
+        in_specs=[pl.BlockSpec(memory_space=pl.ANY), vmem],
+        out_specs=(vmem, vmem),
+        scratch_shapes=[
+            pltpu.VMEM(grad.shape, low),
+            pltpu.VMEM((4, 2, rows, columns), low),
+            pltpu.VMEM((4, rows, columns), low),
+            pltpu.VMEM((3, rows, columns), low),
+            pltpu.VMEM((16,) + small.shape, jnp.float32),
+            dma((n,)), dma((2, n)), dma((2, n)), dma((2, n, 3)), dma((2, 15)),
+        ],
+        compiler_params=pltpu.CompilerParams(collective_id=1, has_side_effects=True, vmem_limit_bytes=50 * 2**20),
+    )(grad, small)
 
 
 def group_norm(values, gain_vec, shift_vec):
@@ -48,7 +228,7 @@
 
 def convolve(source, kernel):
     slot_count = source.shape[0]
-    summed = jnp.zeros((slot_count * PIXELS, kernel.shape[2]), jnp.float32)
+    summed = jnp.zeros((slot_count * PIXELS, kernel[0].shape[1]), jnp.float32)
     for tap_index, window in enumerate(windows(source)):
         summed = summed + jnp.dot(window, kernel[tap_index], preferred_element_type=jnp.float32)
     return summed.reshape(slot_count, PIXELS, -1)
@@ -57,7 +237,7 @@
 def convolve_back(grad_low, kernel):
     slot_count = grad_low.shape[0]
     flattened = grad_low.reshape(slot_count * PIXELS, -1)
-    summed = jnp.zeros((slot_count, SIDE + 2, SIDE + 2, kernel.shape[1]), jnp.float32)
+    summed = jnp.zeros((slot_count, SIDE + 2, SIDE + 2, kernel[0].shape[0]), jnp.float32)
     for tap_index in range(9):
         row_shift = tap_index // 3
         col_shift = tap_index % 3
@@ -78,7 +258,7 @@
         jnp.einsum("rc,rd->cd", window, flattened, preferred_element_type=jnp.float32)
         for window in windows(source)
     ]
-    return jnp.stack(found)
+    return found
 
 
 def gather_features(values_low):
@@ -92,6 +272,7 @@
 
 
 def body(
+    fast,
     images,
     embedding,
     counts,
@@ -107,12 +288,17 @@
     slot_count = images.shape[0]
     score_scale = HEAD_DIM ** (-0.5)
     slot_mask = (jnp.arange(slot_count, dtype=jnp.int32) < counts[0]).astype(jnp.float32)
-    conv_full = lax.all_gather(conv_weights, "dp", axis=2, tiled=True)
-    aff_full, qkv_full, proj_full = (
-        lax.all_gather(aff_weights, "dp", axis=0, tiled=True),
-        lax.all_gather(qkv_weights, "dp", axis=0, tiled=True),
-        lax.all_gather(proj_weights, "dp", axis=0, tiled=True),
-    )
+    width = images.shape[2]
+    if fast:
+        full = gather_weights(conv_weights, aff_weights, qkv_weights, proj_weights).reshape(C, 24, width)
+        conv_full = [[full[:, 9 * part + tap] for tap in range(9)] for part in range(2)]
+        aff_full, qkv_full, proj_full = full[:, 18:20], full[:, 20:23], full[:, 23]
+    else:
+        conv_full = lax.all_gather(conv_weights, "dp", axis=2, tiled=True)
+        aff_full, qkv_full, proj_full = (
+            lax.all_gather(weights, "dp", axis=0, tiled=True)
+            for weights in (aff_weights, qkv_weights, proj_weights)
+        )
     images_f = images.astype(jnp.float32)
     hidden0 = first_norm(images_f, norm_gains[0], norm_shifts[0]).astype(jnp.bfloat16)
     hidden0_all, embed_all = (
@@ -155,12 +341,7 @@
         + lin_biases[4]
     )
     block_output = (slot_mask[:, None, None] * (residual + branch)).astype(jnp.bfloat16)
-    conv_back = lax.all_gather(conv_weights, "dp", axis=2, tiled=True)
-    aff_back, qkv_back, proj_back = (
-        lax.all_gather(aff_weights, "dp", axis=0, tiled=True),
-        lax.all_gather(qkv_weights, "dp", axis=0, tiled=True),
-        lax.all_gather(proj_weights, "dp", axis=0, tiled=True),
-    )
+    conv_back, aff_back, qkv_back, proj_back = conv_full, aff_full, qkv_full, proj_full
     grad_branch = slot_mask[:, None, None] * cotangent
     branch_low = grad_branch.astype(jnp.bfloat16)
     proj_grad = jnp.einsum(
@@ -252,14 +433,25 @@
             aff_bias_grad[1],
         ]
     )
-    gains_grad, shifts_grad, biases_grad = lax.psum((gains_local, shifts_local, biases_local), "dp")
-    conv_local = jnp.stack([conv0_wgrad, conv1_wgrad])
-    conv_summed, aff_summed, qkv_summed, proj_summed = (
-        lax.psum_scatter(conv_local, "dp", scatter_dimension=2, tiled=True),
-        lax.psum_scatter(aff_grad, "dp", scatter_dimension=0, tiled=True),
-        lax.psum_scatter(qkv_grad, "dp", scatter_dimension=0, tiled=True),
-        lax.psum_scatter(proj_grad, "dp", scatter_dimension=0, tiled=True),
-    )
+    if fast:
+        small = jnp.concatenate([gains_local, shifts_local, biases_local, jnp.zeros((3, width), jnp.float32)])
+        parts = conv0_wgrad + conv1_wgrad + [aff_grad.reshape(C, -1), qkv_grad.reshape(C, -1), proj_grad]
+        joined = jnp.concatenate([part.astype(jnp.bfloat16) for part in parts], axis=1)
+        rows = conv_weights.shape[2]
+        summed, totals = scatter_grads(joined.reshape(GRID + (rows, 24 * width)), small)
+        gains_grad, shifts_grad, biases_grad = totals[:3], totals[3:6], totals[6:13]
+        split = summed.reshape(rows, 24, width)
+        conv_summed = split[:, :18].transpose(1, 0, 2).reshape(2, 9, rows, width)
+        aff_summed, qkv_summed, proj_summed = split[:, 18:20], split[:, 20:23], split[:, 23]
+    else:
+        gains_grad, shifts_grad, biases_grad = lax.psum((gains_local, shifts_local, biases_local), "dp")
+        conv_local = jnp.stack([jnp.stack(conv0_wgrad), jnp.stack(conv1_wgrad)])
+        conv_summed, aff_summed, qkv_summed, proj_summed = (
+            lax.psum_scatter(conv_local, "dp", scatter_dimension=2, tiled=True),
+            lax.psum_scatter(aff_grad, "dp", scatter_dimension=0, tiled=True),
+            lax.psum_scatter(qkv_grad, "dp", scatter_dimension=0, tiled=True),
+            lax.psum_scatter(proj_grad, "dp", scatter_dimension=0, tiled=True),
+        )
     return (
         block_output,
         images_grad,
@@ -276,7 +468,7 @@
 
 def solution(mesh):
     return jax.shard_map(
-        body,
+        functools.partial(body, mesh.shape["dp"] == 16),
         mesh=mesh,
         in_specs=(
             P("dp", None, "tensor"),

time: 1110 us -> 885 us (0.80)
  waiting for transfers between devices: 665 us -> 0.15 us
  Pallas kernels: 0 us -> 502 us
  blocking collectives: 136 us -> 12.9 us
  local copies, waits for them, and re-layouts: 116 us -> 229 us
  matrix products: 112 us -> 84.7 us
  other arithmetic: 50.9 us -> 28.3 us
    pallas_call x0 -> x2, Pallas kernels: none -> 502 us  [the longest x1 252 us: scatter_grads(): pl.pallas_call(functools.partial(scatter_kernel, pieces), out_shape=(jax....]
    reduce_scatter x3 -> x0, waiting for transfers between devices: 465 us -> none  [the longest x1 320 us: body(): lax.psum_scatter(conv_local, 'dp', scatter_dimension=2, tiled=True)]
    all_gather x3 -> x0, waiting for transfers between devices: 182 us -> none  [the longest x1 133 us: body(): conv_full = lax.all_gather(conv_weights, 'dp', axis=2, tiled=True)]
    psum x1 -> x0, blocking collectives: 77.9 us -> none  [body(): lax.psum((gains_local, shifts_local, biases_local), 'dp')]
    slice x0 -> x8, local copies, waits for them, and re-layouts: none -> 51.3 us  [the longest x1 41.4 us: body(): full[:, 23]]
    all_gather x1 -> x0, blocking collectives: 45.9 us -> none  [body(): lax.all_gather(proj_weights, 'dp', axis=0, tiled=True)]
    unnamed x244 -> x407, local copies, waits for them, and re-layouts: 65.2 us -> 111 us
    convert_element_type x0 -> x21, local copies, waits for them, and re-layouts: none -> 31.3 us  [body(): part.astype(jnp.bfloat16)]
  transfers between devices with their start and end apart: 12 -> 5, of which waited for: 8 -> 0; matrix products, arithmetic and copies ran while one was open for 13% -> 15% of each run, Pallas kernels for 0% -> 0%
where the time goes in v1:
time: 885 us; the launch traced here: 874 us
  Pallas kernels  502 us (57%)
  local copies, waits for them, and re-layouts  229 us (26%)
  matrix products  84.7 us (10%)
  other arithmetic  28.3 us (3%)
  between operations  17 us (2%)
  blocking collectives  12.9 us (1%)
    pallas_call x1, Pallas kernels, scatter_grads(): pl.pallas_call(functools.partial(scatter_kernel, pieces), out_shape=(jax....  252 us
    pallas_call x1, Pallas kernels, gather_weights(): pl.pallas_call(functools.partial(gather_kernel, pieces), out_shape=jax.Sh...  250 us
    unnamed x407, local copies, waits for them, and re-layouts  111 us
    slice x1, local copies, waits for them, and re-layouts, body(): full[:, 23]  41.4 us
    convert_element_type x21, local copies, waits for them, and re-layouts, body(): part.astype(jnp.bfloat16)  31.3 us
    dot_general x18, matrix products, convolve_back(): jnp.einsum('rd,cd->rc', flattened, kernel[tap_index], preferred_element_t...  22.9 us
    dot_general x18, matrix products, conv_weight_grad(): jnp.einsum('rc,rd->cd', window, flattened, preferred_element_type=jnp.flo...  20.5 us
  transfers between devices with their start and end apart: 5, of which 0 were waited for; matrix products, arithmetic and copies ran while one was open for 15% of the time, Pallas kernels for 0%

profile of v1, /device:TPU:0, one launch (start us, length us, event | category | flops | bytes accessed | tf_op | source)
XLA Modules:
  0.0 874.3 jit_solution(5248544092423976022)
XLA Ops:
  11.0 250.0 %shard_map.186 = bf16[4,2,2,48,9216]{4,3,2,1,0:T(8,128)(2,1)} custom-call(bf16[2,9,48,384]{3,2,1,0:T(8,128)(2,1)} %conv_ref.1, bf16[48,768]{1,0:T(8,128)(2,1)} %bitcast.502, bf16[48,1152]{1,0:T(8,128)(2,1)} %bitcast.495, bf16[48,384]{1,0:T(8,128)(2,1)} %proj_ref.1), custom_call_target="tpu_custom_call" | custom-call | tf_op jit(solution)/shard_map/pallas_call | solution.py:88
  261.0 14.0 %copy.454 = bf16[96,8,24,384]{3,2,1,0:T(8,128)(2,1)} copy(bf16[96,8,24,384]{3,1,2,0:T(8,128)(2,1)} %bitcast.408) | data formatting | bytes 28311552
  275.0 41.4 %fusion.182 = (bf16[768,1,384]{2,1,0:T(2,128)(2,1)S(1)}, bf16[768,1,384]{2,1,0:T(2,128)(2,1)}, bf16[768,1,384]{2,1,0:T(2,128)(2,1)}, bf16[768,1,384]{2,1,0:T(2,1...) fusion(bf16[768,24,384]{2,1,0:T(8,128)(2,1)} %bitcast.405), kind=kLoop, calls=%fused_computation.346 | loop fusion | bytes 22413312 | tf_op jit(solution)/shard_map/slice | solution.py:295
  319.8 3.9 copy.413
  327.0 3.6 slice.301
  334.1 2.7 all_gather.15
  357.7 2.9 all_gather.17
  374.2 3.6 slice.313
  389.9 2.9 reshape.482
  392.8 3.3 convolution_convert_fusion.1
  403.1 3.0 copy.349
  406.0 2.7 stack_reshape.12
  408.7 3.0 copy.353
  411.7 2.7 stack_reshape.13
  414.3 4.4 bitcast_convert_fusion.1
  418.8 4.9 copy.415
  423.7 4.6 reshape.483
  429.6 2.9 convolution_convert_fusion.3
  434.2 2.9 all_gather.19
  441.8 3.3 fusion.13
  445.1 2.8 bitcast_convert_fusion
  448.0 3.9 copy.381
  452.7 2.7 reshape.484
  473.9 4.0 copy.417
  477.9 4.7 reshape.485
  500.3 2.7 reshape.486
  503.0 2.8 copy.418
  505.8 3.4 multiply_reduce_fusion.4
  548.8 4.5 pad_add_fusion
  569.6 3.9 copy.419
  573.5 2.6 reshape.487
  604.1 252.4 %shard_map.187 = (f32[48,9216]{1,0:T(8,128)S(1)}, f32[16,384]{1,0:T(8,128)S(1)}) custom-call(bf16[4,2,2,48,9216]{4,3,2,1,0:T(8,128)(2,1)} %bitcast.428, f32[16,384]{1,0:T(8,128)S(1)} %concatenate.7.small_ref), custom_call_target="tpu_custom_call" | custom-call | tf_op jit(solution)/shard_map/pallas_call | solution.py:176
  (625 shorter events, 204.3 us)
Async XLA Ops:
  7.2 382.7 %reduce-scatter.16.cloned.1.call-start = ((), (), s32[]{:S(2)}) async-start(), calls=%async_computation.5 | async-start | bytes 1474560
  7.9 308.5 %copy-start.175 = (f32[10]{0:T(128)}, f32[10]{0:T(128)S(1)}, u32[]{:S(2)}) copy-start(f32[10]{0:T(128)S(1)} %compare_convert_fusion) | copy-start | bytes 124
  275.0 41.4 %copy-start.8 = (f32[10,64,384]{2,1,0:T(8,128)S(1)}, f32[10,64,384]{2,1,0:T(8,128)}, u32[]{:S(2)}) copy-start(f32[10,64,384]{2,1,0:T(8,128)} %param.21) | copy-start | bytes 2949124
  326.3 6.2 copy-start.5
  326.3 126.3 %reduce-scatter.18.cloned.1.call-start = ((), (), s32[]{:S(2)}) async-start(), calls=%async_computation.6 | async-start | bytes 1474560
  327.0 29.0 %copy-start.159 = (f32[384]{0:T(512)}, f32[384]{0:T(512)S(1)}, u32[]{:S(2)}) copy-start(f32[384]{0:T(512)S(1)} %get-tuple-element.30) | copy-start | bytes 4612
  327.0 6.6 copy-start.179
  327.0 6.7 copy-start.180
  330.6 7.8 copy-start.62
  330.7 22.9 %copy-start.144 = (f32[16,24]{1,0:T(8,128)}, f32[16,24]{1,0:T(8,128)S(1)}, u32[]{:S(2)}) copy-start(f32[16,24]{1,0:T(8,128)S(1)} %add.344) | copy-start | bytes 4612
  333.8 22.3 %copy-start.163 = (f32[384]{0:T(512)}, f32[384]{0:T(512)S(1)}, u32[]{:S(2)}) copy-start(f32[384]{0:T(512)S(1)} %get-tuple-element.97) | copy-start | bytes 4612
  333.8 22.3 %copy-start.165 = (f32[384]{0:T(512)}, f32[384]{0:T(512)S(1)}, u32[]{:S(2)}) copy-start(f32[384]{0:T(512)S(1)} %get-tuple-element.36) | copy-start | bytes 4612
  333.8 40.2 %copy-start.157 = (f32[384]{0:T(512)}, f32[384]{0:T(512)S(1)}, u32[]{:S(2)}) copy-start(f32[384]{0:T(512)S(1)} %get-tuple-element.99) | copy-start | bytes 4612
  336.9 7.2 copy-start.11
  338.5 6.3 copy-start.73
  338.5 7.5 copy-start.75
  338.5 8.3 copy-start.77
  338.5 9.5 %copy-start.79 = (bf16[10,8,8,768]{3,2,1,0:T(8,128)(2,1)}, bf16[10,8,8,768]{3,2,1,0:T(8,128)(2,1)S(1)}, u32[]{:S(2)}) copy-start(bf16[10,8,8,768]{3,2,1,0:T(8,128)(2,1)S(1)} %get-tuple-element.77) | copy-start | bytes 2949124
  338.8 17.2 %copy-start.131 = (f32[10,384]{1,0:T(8,128)}, f32[10,384]{1,0:T(8,128)S(1)}, u32[]{:S(2)}) copy-start(f32[10,384]{1,0:T(8,128)S(1)} %get-tuple-element.85) | copy-start | bytes 46084
  338.9 17.2 %copy-start.142 = (f32[10,384]{1,0:T(8,128)}, f32[10,384]{1,0:T(8,128)S(1)}, u32[]{:S(2)}) copy-start(f32[10,384]{1,0:T(8,128)S(1)} %get-tuple-element.86) | copy-start | bytes 46084
  355.8 6.4 copy-start.135
  360.6 7.1 copy-start.13
  362.2 6.2 copy-start.87
  362.2 7.4 copy-start.85
  362.3 8.2 copy-start.83
  362.3 9.4 %copy-start.81 = (bf16[10,8,8,768]{3,2,1,0:T(8,128)(2,1)}, bf16[10,8,8,768]{3,2,1,0:T(8,128)(2,1)S(1)}, u32[]{:S(2)}) copy-start(bf16[10,8,8,768]{3,2,1,0:T(8,128)(2,1)S(1)} %get-tuple-element.69) | copy-start | bytes 2949124
  372.9 86.4 %copy-start.2 = (f32[10,64,384]{2,1,0:T(8,128)}, f32[10,64,384]{2,1,0:T(8,128)S(1)}, u32[]{:S(2)}) copy-start(f32[10,64,384]{2,1,0:T(8,128)S(1)} %get-tuple-element.46) | copy-start | bytes 2949124
  428.3 71.9 %reduce-scatter.20.cloned.1.call-start = ((), (), s32[]{:S(2)}) async-start(), calls=%async_computation.7 | async-start | bytes 1474560
  482.6 114.3 %reduce-scatter.24.cloned.1.call-start = ((), (), s32[]{:S(2)}) async-start(), calls=%async_computation.9 | async-start | bytes 294912
  503.0 6.5 copy-start.152
  503.0 6.6 copy-start.1
  548.7 49.9 %reduce-scatter.22.cloned.1.call-start = ((), (), s32[]{:S(2)}) async-start(), calls=%async_computation.8 | async-start | bytes 1474560
  (155 other events, 458.2 us)
Sparse Core Ops, SparseCore 0:
  326.5 17.2 reduce-scatter.15
  428.4 17.1 reduce-scatter.17
  482.7 16.8 reduce-scatter.19
  548.9 16.0 reduce-scatter.23
  576.3 16.9 reduce-scatter.21
